TPU v7x, 256 devices: a whole 4x4x8 slice. The times are simulated.
256 devices in a mesh: seq: 64 (over y, z, core), fsdp: 4 (over x).
Axes of the slice: x: 4, y: 4, z: 8, core: 2. Of those that a mesh axis runs over, the one named last changes fastest.
Arguments:
- tokens: bfloat16 [65536, 4096], P('seq', 'fsdp'), may hold values from -6 to 6
- projection: bfloat16 [3, 4096, 2048], P(None, 'seq', 'fsdp'), may hold values from -0.09375 to 0.09375
- log_decay: float32 [65536, 16], P('seq', 'fsdp'), may hold values from -2 to 0, as said below
Outputs:
- attended: bfloat16 [65536, 2048], P('seq', 'fsdp')
Inputs may be any that keep to these rules, and one draw needn't show every extreme that they name: `log_decay`: negative logarithms of decay factors, one for each position and head.
All inputs are finite; a program needn't handle non-finite values.
Results may differ from a plain program's by a relative error of at most 0.006.
Values may be sent and summed in bfloat16 or wider, within the bound.
No kernel may reach another device: no remote copies, remote signals or barrier semaphores. Data moves between devices by JAX's collectives and lax.ppermute only.
A program may use at most 64 MiB of HBM per device.

v0:
```python
import jax
import jax.numpy as jnp
from jax import lax
from jax.sharding import PartitionSpec as P

BLK = 512


def entering(part, axis, combine, identity):
    place = lax.axis_index(axis)
    gathered = jax.tree.map(lambda a: lax.all_gather(a, axis), part)
    state = jax.tree.map(lambda a, e: jnp.zeros_like(a) + jnp.asarray(e, a.dtype), part, identity)

    def one(hop, state):
        return combine(
            state, jax.tree.map(lambda a: lax.dynamic_index_in_dim(a, hop, 0, False), gathered)
        )

    return lax.fori_loop(0, place, one, state)


def local_states(key_vecs, value_vecs, decay):
    running = jnp.cumsum(decay, axis=1)
    last = running[:, -1]
    carried = key_vecs.astype(jnp.float32) * jnp.exp(last[:, None, :] - running)[..., None]
    fresh = jnp.einsum(
        "nshd,nshe->nhde", carried, value_vecs.astype(jnp.float32), precision=lax.Precision.HIGHEST
    )

    def advance(state, inputs):
        block_last, block_fresh = inputs
        return (jnp.exp(block_last)[:, None, None] * state + block_fresh, state)

    start = jnp.zeros(fresh.shape[1:], jnp.float32)
    final, before = lax.scan(advance, start, (last, fresh))
    leading = jnp.cumsum(last, axis=0) - last
    whole_decay = jnp.exp(jnp.sum(last, axis=0))
    return (final, before, leading, whole_decay)


def combine(earlier, later):
    return (earlier[0] * later[0], later[0][:, None, None] * earlier[1] + later[1])


def chain(key_raw, value_raw, decay, shaped):
    key_vecs = shaped(jax.nn.silu(key_raw).astype(jnp.bfloat16))
    value_vecs = shaped(value_raw.astype(jnp.bfloat16))
    final, before, leading, whole_decay = local_states(key_vecs, value_vecs, decay)
    identity = (jnp.ones_like(whole_decay), jnp.zeros_like(final))
    carry = entering((whole_decay, final), "seq", combine, identity)
    incoming = before + jnp.exp(leading)[:, :, None, None] * carry[1][None]
    return (key_vecs, value_vecs, incoming)


def attend_block(inputs):
    queries, key_vecs, value_vecs, decay, state = inputs
    running = jnp.cumsum(decay, axis=0)
    across = running.T
    gap = across[:, :, None] - across[:, None, :]
    lower = jnp.arange(gap.shape[1])[:, None] >= jnp.arange(gap.shape[2])[None, :]
    fading = jnp.exp(jnp.where(lower[None], gap, -1e30))
    scores = jnp.einsum("thd,shd->hts", queries, key_vecs, preferred_element_type=jnp.float32)
    weights = (fading * scores).astype(jnp.bfloat16)
    intra = jnp.einsum("hts,she->the", weights, value_vecs, preferred_element_type=jnp.float32)
    inter = jnp.exp(running)[:, :, None] * jnp.einsum(
        "thd,hde->the", queries.astype(jnp.float32), state, precision=lax.Precision.HIGHEST
    )
    mixed = intra + inter
    normed = mixed * lax.rsqrt(jnp.mean(mixed * mixed, axis=-1, keepdims=True) + 1e-06)
    return normed.astype(jnp.bfloat16)


def on_device(tokens, projection, log_decay):
    features = lax.all_gather(tokens, "fsdp", axis=1, tiled=True)
    rows = features.shape[0]
    heads = log_decay.shape[1]
    width = projection.shape[2]
    head = width // heads
    blocks = rows // BLK

    def shaped(matrix):
        return matrix.reshape(blocks, BLK, heads, head)

    decay = log_decay.reshape(blocks, BLK, heads)
    raw = jnp.einsum(
        "td,cdn->ctn",
        features,
        lax.all_gather(projection, "seq", axis=1, tiled=True),
        preferred_element_type=jnp.float32,
    )
    key_vecs, value_vecs, incoming = chain(raw[1], raw[2], decay, shaped)
    query_raw = raw[0]
    queries = shaped(jax.nn.silu(query_raw).astype(jnp.bfloat16))
    outputs = lax.map(attend_block, (queries, key_vecs, value_vecs, decay, incoming))
    return outputs.reshape(rows, width)


def solution(mesh):
    in_specs = (P("seq", "fsdp"), P(None, "seq", "fsdp"), P("seq", "fsdp"))
    out_specs = P("seq", "fsdp")
    return jax.shard_map(
        on_device, mesh=mesh, in_specs=in_specs, out_specs=out_specs, check_vma=False
    )
```

profile of v0, /device:TPU:249, one launch (start us, length us, event | category | flops | bytes accessed | tf_op | source)
XLA Modules:
  0.0 447.1 jit_solution(9601108571453135276)
XLA Ops:
  8.1 2.4 reduce-window.14
  11.5 83.5 %all-gather.8.cloned.1.call-done = bf16[1024,4096]{1,0:T(8,128)(2,1)} async-done(((bf16[1024,1024]{1,0:T(8,128)(2,1)}), bf16[1024,4096]{1,0:T(8,128)(2,1)}) %all-gather.8.cloned.1.call-update) | async-done | bytes 8388624 | tf_op jit(solution)/shard_map/all_gather | solution.py:74
  95.0 90.9 %all-gather.6.cloned.1.call-done = bf16[3,4096,512]{2,1,0:T(8,128)(2,1)} async-done(((bf16[3,64,512]{2,1,0:T(8,128)(2,1)}), bf16[3,4096,512]{2,1,0:T(8,128)(2,1)}) %all-gather.6.cloned.1.call-update) | async-done | bytes 12582928 | tf_op jit(solution)/shard_map/all_gather | solution.py:88
  185.9 17.3 %fusion.27 = f32[3,1024,512]{1,2,0:T(8,128)S(1)} fusion(bf16[3,4096,512]{2,1,0:T(8,128)(2,1)} %all-gather.6.cloned.1.call-done, bf16[1024,4096]{1,0:T(8,128)(2,1)} %all-gather.8.cloned.1.call-done), kind=kOutput, calls=%fused_computation.39 | convolution fusion | flops 12884901888 | bytes 27262976 | tf_op jit(solution)/shard_map/td,cdn->ctn/dot_general | solution.py:85
  203.3 1.8 fusion.35
  205.1 1.6 convert_element_type.24
  206.7 2.8 squeeze.42
  209.4 2.8 copy.51
  212.2 4.0 squeeze.41
  216.2 4.1 copy.49
  220.3 2.8 multiply_convert_fusion.2
  223.1 2.7 fusion.30
  228.3 124.5 %all-reduce = f32[256]{0:T(256)S(1)} all-reduce(f32[256]{0:T(256)S(1)} %exponential_dynamic-update-slice_fusion), channel_id=2, replica_groups=mesh['seq'=64,'fsdp'=4] {'seq'}, use_global_device_ids=true, to_apply=%add | all-reduce | flops 256 | bytes 2048
  353.0 1.2 copy.54
  354.2 69.7 %while.35 = (s32[]{:T(128)}, f32[4,128,128]{2,1,0:T(8,128)S(1)}, s32[]{:T(128)}, f32[64,4]{1,0:T(8,128)S(1)}, f32[64,4,128,128]{3,2,1,0:T(8,128)}, /*index=5*/s32[]{:T(128)}, s32[]{:T(128)}, s32[]{:T(128)}) while((s32[]{:T(128)}, f32[4,128,128]{2,1,0:T(8,128)S(1)}, s32[]{:T(128)}, f32[64,4]{1,0:T(8,128)S(1)}, f32[64,4,128,128]{3,2,1,0:T(8,128)}, ...), condition=%wide.region_7.8_spmd, body=%wide.region_6.7_spmd.sunk | while | flops 131077 | bytes 786615 | solution.py:19
  354.2 1.1 bitcast_add_fusion.4
  355.3 1.1 bitcast_add_fusion.4
  356.4 1.1 bitcast_add_fusion.4
  357.5 1.1 bitcast_add_fusion.4
  358.6 1.1 bitcast_add_fusion.4
  359.7 1.1 bitcast_add_fusion.4
  364.1 1.1 bitcast_add_fusion.4
  365.2 1.1 bitcast_add_fusion.4
  366.3 1.1 bitcast_add_fusion.4
  367.4 1.1 bitcast_add_fusion.4
  368.5 1.1 bitcast_add_fusion.4
  369.6 1.1 bitcast_add_fusion.4
  375.2 1.1 bitcast_add_fusion.4
  376.3 1.1 bitcast_add_fusion.4
  377.4 1.1 bitcast_add_fusion.4
  378.5 1.1 bitcast_add_fusion.4
  379.6 1.1 bitcast_add_fusion.4
  380.7 1.1 bitcast_add_fusion.4
  385.1 1.1 bitcast_add_fusion.4
  386.2 1.1 bitcast_add_fusion.4
  387.3 1.1 bitcast_add_fusion.4
  388.4 1.1 bitcast_add_fusion.4
  389.5 1.1 bitcast_add_fusion.4
  390.6 1.1 bitcast_add_fusion.4
  396.1 1.1 bitcast_add_fusion.4
  397.2 1.1 bitcast_add_fusion.4
  398.3 1.1 bitcast_add_fusion.4
  424.0 14.2 %while.36 = (s32[]{:T(128)}, bf16[2,512,4,128]{3,2,1,0:T(4,128)(2,1)}, bf16[2,512,4,128]{1,3,2,0:T(8,128)(2,1)}, f32[2,512,4]{1,2,0:T(4,128)S(1)}, bf16[2,512,4,...) while((s32[]{:T(128)}, ...), condition=%wide.region_12.13_spmd, body=%wide.region_8.12_spmd.sunk | while | flops 945817664 | bytes 9857989 | solution.py:94
  424.0 1.2 reduce-window.24
  425.8 3.1 fusion.46
  431.1 1.2 reduce-window.24
  432.9 3.1 fusion.46
  438.2 2.4 copy.70
  (172 shorter events, 49.3 us)
Async XLA Ops:
  6.5 1.5 copy-start.5
  6.5 88.4 %all-gather.8.cloned.1.call-start = ((), (), s32[]{:S(2)}) async-start(), calls=%async_computation.1 | async-start | bytes 10485760 | tf_op jit(solution)/shard_map/all_gather | solution.py:74
  7.3 178.6 %all-gather.6.cloned.1.call-start = ((), (), s32[]{:S(2)}) async-start(), calls=%async_computation | async-start | bytes 12779520 | tf_op jit(solution)/shard_map/all_gather | solution.py:88
  8.0 346.1 %all-gather.10.cloned.1.call-start = ((), (), s32[]{:S(2)}) async-start(), calls=%async_computation.2 | async-start | bytes 17039360 | tf_op jit(solution)/shard_map/all_gather | solution.py:11
  220.3 2.8 copy-start.1
  223.1 2.8 copy-start.3
  223.1 2.8 copy-start.4
  225.9 1.2 copy-start.6
  225.9 127.1 %copy-start.2 = (bf16[2,512,4,128]{1,0,3,2:T(2,128)(2,1)S(1)}, bf16[2,512,4,128]{1,0,3,2:T(2,128)(2,1)}, u32[]{:S(2)}) copy-start(bf16[2,512,4,128]{1,0,3,2:T(2,128)(2,1)} %convert_element_type.24) | copy-start | bytes 3145732
  226.3 0.7 copy-start
Sparse Core Ops, SparseCore 0:
  9.2 85.7 all-gather.7
  97.8 88.0 all-gather.5
  227.1 96.5 all-gather.9
where the time goes:
time: 449 us; the launch traced here: 447 us
  waiting for transfers between devices  176 us (39%)
  blocking collectives  125 us (28%)
  other arithmetic  76.6 us (17%)
  matrix products  27.7 us (6%)
  local copies, waits for them, and re-layouts  26.2 us (6%)
  between operations  13.9 us (3%)
    unnamed x1, blocking collectives  125 us
    all_gather x1, waiting for transfers between devices, on_device(): lax.all_gather(projection, 'seq', axis=1, tiled=True)  90.9 us
    all_gather x1, waiting for transfers between devices, on_device(): features = lax.all_gather(tokens, 'fsdp', axis=1, tiled=True)  83.5 us
    add x63, other arithmetic, combine(): later[0][:, None, None] * earlier[1] + later[1]  66.8 us
    dot_general x1, matrix products, on_device(): jnp.einsum('td,cdn->ctn', features, lax.all_gather(projection, 'seq', axi...  17.3 us
  transfers between devices with their start and end apart: 3, of which 2 were waited for; matrix products, arithmetic and copies ran while one was open for 1% of the time, Pallas kernels for 0%

commit v1 on v0

--- a/solution.py
+++ b/solution.py
@@ -71,7 +71,9 @@
 
 
 def on_device(tokens, projection, log_decay):
-    features = lax.all_gather(tokens, "fsdp", axis=1, tiled=True)
+    features = jnp.concatenate(
+        lax.all_to_all(jnp.stack([tokens] * lax.axis_size("fsdp")), "fsdp", 0, 0), axis=1
+    )
     rows = features.shape[0]
     heads = log_decay.shape[1]
     width = projection.shape[2]

time: 449 us -> 403 us (0.90)
  waiting for transfers between devices: 176 us -> 90.5 us
  local copies, waits for them, and re-layouts: 26.2 us -> 58.7 us
  starting transfers between devices: 0.08 us -> 5.84 us
    all_gather x1, waiting for transfers between devices: 90.9 us -> 0.01 us  [on_device(): lax.all_gather(projection, 'seq', axis=1, tiled=True)]
    all_to_all x0 -> x1, waiting for transfers between devices: none -> 89.7 us  [on_device(): lax.all_to_all(jnp.stack([tokens] * lax.axis_size('fsdp')), 'fsdp', 0, 0)]
    all_gather x1 -> x0, waiting for transfers between devices: 83.5 us -> none  [on_device(): features = lax.all_gather(tokens, 'fsdp', axis=1, tiled=True)]
    reshape x2 -> x4, local copies, waits for them, and re-layouts: 0.03 us -> 26.6 us  [the longest x2 26.6 us: on_device(): jnp.concatenate(lax.all_to_all(jnp.stack([tokens] * lax.axis_size('fsdp')...]
    another operation x4 -> x5, local copies, waits for them, and re-layouts: 0.22 us -> 6.29 us  [the longest x1 6.07 us: on_device(): jnp.stack([tokens] * lax.axis_size('fsdp'))]
    all_to_all x0 -> x1, starting transfers between devices: none -> 5.79 us  [on_device(): lax.all_to_all(jnp.stack([tokens] * lax.axis_size('fsdp')), 'fsdp', 0, 0)]
  transfers between devices with their start and end apart: 3 -> 3, of which waited for: 2 -> 1; matrix products, arithmetic and copies ran while one was open for 1% -> 9% of each run, Pallas kernels for 0% -> 0%
where the time goes in v1:
time: 403 us; the launch traced here: 401 us
  blocking collectives  124 us (31%)
  waiting for transfers between devices  90.5 us (22%)
  other arithmetic  76.6 us (19%)
  local copies, waits for them, and re-layouts  58.7 us (15%)
  matrix products  27.7 us (7%)
  between operations  14.3 us (4%)
  starting transfers between devices  5.84 us (1%)
    unnamed x1, blocking collectives  124 us
    all_to_all x1, waiting for transfers between devices, on_device(): lax.all_to_all(jnp.stack([tokens] * lax.axis_size('fsdp')), 'fsdp', 0, 0)  89.7 us
    add x63, other arithmetic, combine(): later[0][:, None, None] * earlier[1] + later[1]  66.8 us
    reshape x2, local copies, waits for them, and re-layouts, on_device(): jnp.concatenate(lax.all_to_all(jnp.stack([tokens] * lax.axis_size('fsdp')...  26.6 us
    dot_general x1, matrix products, on_device(): jnp.einsum('td,cdn->ctn', features, lax.all_gather(projection, 'seq', axi...  17.3 us
    squeeze x2, local copies, waits for them, and re-layouts, on_device(): key_vecs, value_vecs, incoming = chain(raw[1], raw[2], decay, shaped)  8.14 us
  transfers between devices with their start and end apart: 3, of which 1 were waited for; matrix products, arithmetic and copies ran while one was open for 9% of the time, Pallas kernels for 0%

profile of v1, /device:TPU:249, one launch (start us, length us, event | category | flops | bytes accessed | tf_op | source)
XLA Modules:
  0.0 400.6 jit_solution(9774965457901973969)
XLA Ops:
  7.3 6.1 %stack.2 = bf16[4,1024,1024]{2,1,0:T(8,128)(2,1)} broadcast(bf16[1024,1024]{1,0:T(8,128)(2,1)} %param.9), dimensions={1,2} | broadcast | bytes 10485760 | tf_op jit(solution)/shard_map/stack | solution.py:75
  13.3 5.8 %all-to-all-start = ((bf16[4,1024,1024]{2,1,0:T(8,128)(2,1)}), bf16[4,1024,1024]{2,1,0:T(8,128)(2,1)}, u32[]{:S(2)}, u32[]{:S(2)}) async-start(bf16[4,1024,1024]{2,1,0:T(8,128)(2,1)} %stack.2), calls=%async_computation | async-start | bytes 16777216 | tf_op jit(solution)/shard_map/all_to_all | solution.py:75
  19.2 2.4 reduce-window.14
  22.6 89.7 %all-to-all-done = bf16[4,1024,1024]{2,1,0:T(8,128)(2,1)} async-done(((bf16[4,1024,1024]{2,1,0:T(8,128)(2,1)}), bf16[4,1024,1024]{2,1,0:T(8,128)(2,1)}, u32[]{:S(2)}, u32[]{:S(2)}) %all-to-all-start) | async-done | bytes 8388640 | tf_op jit(solution)/shard_map/all_to_all | solution.py:75
  112.3 12.1 %copy.50 = bf16[1024,4,1024]{2,1,0:T(4,128)(2,1)} copy(bf16[1024,4,1024]{2,0,1:T(8,128)(2,1)} %bitcast.12) | data formatting | bytes 16777216 | tf_op jit(solution)/shard_map/reshape | solution.py:74
  124.5 14.4 %reshape.127 = bf16[1024,4096,1]{1,0,2:T(8,128)(2,1)} reshape(bf16[1024,4,1024]{2,1,0:T(4,128)(2,1)} %copy.50) | data formatting | bytes 16777216 | tf_op jit(solution)/shard_map/reshape | solution.py:74
  138.9 17.3 %convolution_bitcast_fusion.1 = f32[3,1024,512]{1,2,0:T(8,128)S(1)} fusion(bf16[3,4096,512]{2,1,0:T(8,128)(2,1)} %all-gather.5.cloned.1.call-done, bf16[1024,4096,1]{1,0,2:T(8,128)(2,1)} %reshape.127), kind=kOutput, calls=%fused_computation.37 | convolution fusion | flops 12884901888 | bytes 27262976 | tf_op jit(solution)/shard_map/td,cdn->ctn/dot_general | solution.py:87
  156.2 1.8 fusion.30
  158.1 2.8 squeeze.41
  160.9 2.8 copy.52
  163.7 4.0 squeeze.42
  167.7 4.1 %copy.54 = f32[2,512,4,128]{3,1,2,0:T(8,128)} copy(f32[2,512,4,128]{1,0,3,2:T(2,128)} %squeeze.42) | data formatting | bytes 4194304 | tf_op jit(solution)/shard_map/squeeze | solution.py:93
  171.8 1.6 convert_element_type.24
  173.4 2.8 multiply_convert_fusion.2
  176.2 2.7 fusion.25
  181.4 124.5 %all-reduce = f32[256]{0:T(256)S(1)} all-reduce(f32[256]{0:T(256)S(1)} %exponential_dynamic-update-slice_fusion), channel_id=2, replica_groups=mesh['seq'=64,'fsdp'=4] {'seq'}, use_global_device_ids=true, to_apply=%add | all-reduce | flops 256 | bytes 2048
  306.0 1.2 copy.57
  307.2 69.9 %while.35 = (s32[]{:T(128)}, f32[4,128,128]{2,1,0:T(8,128)S(1)}, s32[]{:T(128)}, f32[64,4]{1,0:T(8,128)S(1)}, f32[64,4,128,128]{3,2,1,0:T(8,128)}, /*index=5*/s32[]{:T(128)}, s32[]{:T(128)}, s32[]{:T(128)}) while((s32[]{:T(128)}, f32[4,128,128]{2,1,0:T(8,128)S(1)}, s32[]{:T(128)}, f32[64,4]{1,0:T(8,128)S(1)}, f32[64,4,128,128]{3,2,1,0:T(8,128)}, ...), condition=%wide.region_7.8_spmd, body=%wide.region_6.7_spmd.sunk | while | flops 131077 | bytes 786607 | solution.py:19
  307.2 1.1 bitcast_add_fusion.4
  309.5 1.1 bitcast_add_fusion.4
  311.7 1.1 bitcast_add_fusion.4
  313.9 1.1 bitcast_add_fusion.4
  316.1 1.1 bitcast_add_fusion.4
  318.3 1.1 bitcast_add_fusion.4
  319.4 1.1 bitcast_add_fusion.4
  320.5 1.1 bitcast_add_fusion.4
  321.6 1.1 bitcast_add_fusion.4
  322.7 1.1 bitcast_add_fusion.4
  323.8 1.1 bitcast_add_fusion.4
  326.0 1.1 bitcast_add_fusion.4
  328.3 1.1 bitcast_add_fusion.4
  330.5 1.1 bitcast_add_fusion.4
  332.7 1.1 bitcast_add_fusion.4
  334.9 1.1 bitcast_add_fusion.4
  337.1 1.1 bitcast_add_fusion.4
  339.3 1.1 bitcast_add_fusion.4
  340.4 1.1 bitcast_add_fusion.4
  341.5 1.1 bitcast_add_fusion.4
  342.6 1.1 bitcast_add_fusion.4
  343.7 1.1 bitcast_add_fusion.4
  344.8 1.1 bitcast_add_fusion.4
  347.1 1.1 bitcast_add_fusion.4
  377.2 14.2 %while.36 = (s32[]{:T(128)}, bf16[2,512,4,128]{3,2,1,0:T(4,128)(2,1)}, bf16[2,512,4,128]{1,3,2,0:T(8,128)(2,1)}, f32[2,512,4]{1,2,0:T(4,128)S(1)}, bf16[2,512,4,...) while((s32[]{:T(128)}, ...), condition=%wide.region_12.13_spmd, body=%wide.region_8.12_spmd.sunk | while | flops 945817664 | bytes 9858489 | solution.py:96
  377.2 1.2 reduce-window.24
  379.0 3.1 fusion.42
  384.3 1.2 reduce-window.24
  386.0 3.1 fusion.42
  391.4 2.4 copy.73
  (174 shorter events, 51.6 us)
Async XLA Ops:
  6.5 132.4 %all-gather.5.cloned.1.call-start = ((), (), s32[]{:S(2)}) async-start(), calls=%async_computation.1 | async-start | bytes 12779520 | tf_op jit(solution)/shard_map/all_gather | solution.py:90
  13.3 5.9 %copy-start.5 = (f32[1024,4]{0,1:T(4,128)S(1)}, f32[1024,4]{0,1:T(4,128)}, u32[]{:S(2)}) copy-start(f32[1024,4]{0,1:T(4,128)} %param.11) | copy-start | bytes 49156
  13.3 99.0 %all-to-all-start = ((bf16[4,1024,1024]{2,1,0:T(8,128)(2,1)}), bf16[4,1024,1024]{2,1,0:T(8,128)(2,1)}, u32[]{:S(2)}, u32[]{:S(2)}) async-start(bf16[4,1024,1024]{2,1,0:T(8,128)(2,1)} %stack.2), calls=%async_computation | async-start | bytes 16777216 | tf_op jit(solution)/shard_map/all_to_all | solution.py:75
  19.1 288.1 %all-gather.7.cloned.1.call-start = ((), (), s32[]{:S(2)}) async-start(), calls=%async_computation.2 | async-start | bytes 17039360 | tf_op jit(solution)/shard_map/all_gather | solution.py:11
  173.4 2.8 copy-start.1
  176.1 2.8 copy-start.3
  176.1 2.8 copy-start.4
  178.9 1.2 copy-start.6
  178.9 127.1 %copy-start.2 = (bf16[2,512,4,128]{1,0,3,2:T(2,128)(2,1)S(1)}, bf16[2,512,4,128]{1,0,3,2:T(2,128)(2,1)}, u32[]{:S(2)}) copy-start(bf16[2,512,4,128]{1,0,3,2:T(2,128)(2,1)} %convert_element_type.24) | copy-start | bytes 3145732
  179.3 0.7 copy-start
Sparse Core Ops, SparseCore 0:
  10.2 87.2 all-gather.4
  180.1 95.8 all-gather.6
